TPU v7x, 256 devices: a whole 4x4x8 slice. The times are simulated.
256 devices in a mesh: dp: 4 (over y), depth: 4 (over x), grid: 16 (over z, core).
Axes of the slice: x: 4, y: 4, z: 8, core: 2. Of those that a mesh axis runs over, the one named last changes fastest.
Arguments:
- tokens: bfloat16 [1024, 12288], P(('dp', 'depth'), 'grid'), may hold values from -6 to 6
- weight: bfloat16 [12288, 24576], P('grid', 'depth'), may hold values from -0.0546875 to 0.0546875
- cotangent: bfloat16 [1024, 24576], P(('dp', 'grid'), 'depth'), may hold values from -0.5 to 0.5
Outputs:
- hidden: bfloat16 [1024, 24576], P(('dp', 'grid'), 'depth')
- weight_grad: bfloat16 [12288, 24576], P(('grid', 'dp'), 'depth')
All inputs are finite; a program needn't handle non-finite values.
Results may differ from a plain program's by a relative error of at most 0.011.
Values may be sent and summed in bfloat16 or wider, within the bound.
A program may use at most 64 MiB of HBM per device.

v0:
```python
import jax
import jax.numpy as jnp
from jax import lax
from jax.sharding import PartitionSpec as P


def gelu_tanh(values):
    return jax.nn.gelu(values, approximate=True)


def transposed_product(left, right):
    return lax.dot_general(
        left, right, (((0,), (0,)), ((), ())), preferred_element_type=jnp.float32
    )


def local(tokens, weight, cotangent):
    all_rows = lax.all_gather(tokens, ("dp", "depth"), axis=0, tiled=True)
    group_size = all_rows.shape[0] // lax.axis_size("dp")
    own_rows = lax.dynamic_slice_in_dim(all_rows, lax.axis_index("dp") * group_size, group_size, 0)
    partial_pre = jnp.dot(own_rows, weight, preferred_element_type=jnp.float32)
    preact = lax.psum_scatter(partial_pre, "grid", scatter_dimension=0, tiled=True)
    activated, pullback = jax.vjp(gelu_tanh, preact)
    hidden = activated.astype(jnp.bfloat16)
    grad_pre = pullback(cotangent.astype(jnp.float32))[0].astype(jnp.bfloat16)
    sub_width = all_rows.shape[1] // lax.axis_size("dp")
    columns = lax.dynamic_slice_in_dim(all_rows, lax.axis_index("dp") * sub_width, sub_width, 1)
    weight_grad = transposed_product(
        columns, lax.all_gather(grad_pre, ("dp", "grid"), axis=0, tiled=True)
    )
    return (hidden, weight_grad.astype(jnp.bfloat16))


def solution(mesh):
    return jax.shard_map(
        local,
        mesh=mesh,
        in_specs=(P(("dp", "depth"), "grid"), P("grid", "depth"), P(("dp", "grid"), "depth")),
        out_specs=(P(("dp", "grid"), "depth"), P(("grid", "dp"), "depth")),
        check_vma=False,
    )
```

profile of v0, /device:TPU:1, one launch (start us, length us, event | category | flops | bytes accessed | tf_op | source)
XLA Modules:
  0.0 246.5 jit_solution(15695499243250786414)
XLA Ops:
  7.2 0.0 all-gather.3.cloned.1.call-start
  7.2 0.7 all-gather.3.cloned.1.call-update
  7.9 0.0 reduce-scatter.2.cloned.1.call-start
  7.9 54.3 %all-gather.3.cloned.1.call-done = bf16[1024,768]{1,0:T(8,128)(2,1)} async-done(((bf16[64,768]{1,0:T(8,128)(2,1)}), bf16[1024,768]{1,0:T(8,128)(2,1)}) %all-gather.3.cloned.1.call-update) | async-done | bytes 1572880 | tf_op jit(solution)/shard_map/all_gather | solution.py:18
  62.3 9.1 %fusion.11 = f32[256,6144]{1,0:T(8,128)} fusion(bf16[768,6144]{1,0:T(8,128)(2,1)} %param.4, bf16[1024,768]{1,0:T(8,128)(2,1)} %all-gather.3.cloned.1.call-done, s32[]{:T(128)S(6)} %select_n.6), kind=kOutput, calls=%fused_computation.17 | convolution fusion | flops 2415919104 | bytes 16121860 | tf_op jit(solution)/shard_map/dot_general | solution.py:21
  71.4 0.0 copy-start
  71.4 0.0 reduce-scatter.2.cloned.1.call-update
  71.4 0.0 all-gather.5.cloned.1.call-start
  71.5 64.0 %reduce-scatter.2.cloned.1.call-done = f32[16,6144]{1,0:T(8,128)} async-done(((f32[256,6144]{1,0:T(8,128)}), f32[16,6144]{1,0:T(8,128)}) %reduce-scatter.2.cloned.1.call-update) | async-done | bytes 393232 | tf_op jit(solution)/shard_map/reduce_scatter | solution.py:22
  135.4 0.0 copy-done
  135.4 2.0 fusion.3
  137.5 0.0 all-gather.5.cloned.1.call-update
  137.5 93.4 %all-gather.5.cloned.1.call-done = bf16[1024,6144]{1,0:T(8,128)(2,1)} async-done(((bf16[16,6144]{1,0:T(8,128)(2,1)}), bf16[1024,6144]{1,0:T(8,128)(2,1)}) %all-gather.5.cloned.1.call-update) | async-done | bytes 12582928 | tf_op jit(solution)/shard_map/all_gather | solution.py:29
  230.9 9.0 %convolution_convert_fusion = bf16[192,6144]{1,0:T(8,128)(2,1)} fusion(bf16[1024,6144]{1,0:T(8,128)(2,1)} %all-gather.5.cloned.1.call-done, bf16[1024,768]{1,0:T(8,128)(2,1)} %all-gather.3.cloned.1.call-done, s32[]{:T(128)S(6)} %select_n.7), kind=kOutput, calls=%fused_computation | convolution fusion | flops 2417098752 | bytes 15466500 | tf_op jit(solution)/shard_map/dot_general | solution.py:12
Async XLA Ops:
  7.2 55.1 %all-gather.3.cloned.1.call-start = ((), (), s32[]{:S(2)}) async-start(), calls=%async_computation.1 | async-start | bytes 1671168 | tf_op jit(solution)/shard_map/all_gather | solution.py:18
  7.9 127.5 %reduce-scatter.2.cloned.1.call-start = ((), (), s32[]{:S(2)}) async-start(), calls=%async_computation.2 | async-start | bytes 6684672 | tf_op jit(solution)/shard_map/reduce_scatter | solution.py:22
  71.4 64.1 %copy-start = (bf16[16,6144]{1,0:T(8,128)(2,1)S(1)}, bf16[16,6144]{1,0:T(8,128)(2,1)}, u32[]{:S(2)}) copy-start(bf16[16,6144]{1,0:T(8,128)(2,1)} %param.5) | copy-start | bytes 589828
  71.4 159.5 %all-gather.5.cloned.1.call-start = ((), (), s32[]{:S(2)}) async-start(), calls=%async_computation.3 | async-start | bytes 12779520 | tf_op jit(solution)/shard_map/all_gather | solution.py:29
Sparse Core Ops, SparseCore 0:
  10.4 51.8 all-gather.2
  71.5 63.8 reduce-scatter.1
  138.8 92.1 all-gather.4
where the time goes:
time: 247 us; the launch traced here: 246 us
  waiting for transfers between devices  212 us (86%)
  matrix products  18.1 us (7%)
  between operations  13.8 us (6%)
    all_gather x1, waiting for transfers between devices, local(): lax.all_gather(grad_pre, ('dp', 'grid'), axis=0, tiled=True)  93.4 us
    reduce_scatter x1, waiting for transfers between devices, local(): lax.psum_scatter(partial_pre, 'grid', scatter_dimension=0, tiled=True)  64 us
    all_gather x1, waiting for transfers between devices, local(): all_rows = lax.all_gather(tokens, ('dp', 'depth'), axis=0, tiled=True)  54.3 us
    dot_general x1, matrix products, local(): partial_pre = jnp.dot(own_rows, weight, preferred_element_type=jnp.float32)  9.11 us
    dot_general x1, matrix products, transposed_product(): lax.dot_general(left, right, (((0,), (0,)), ((), ())), preferred_element_...  9.03 us
  transfers between devices with their start and end apart: 3, of which 3 were waited for; matrix products, arithmetic and copies ran while one was open for 0% of the time, Pallas kernels for 0%

commit v1 on v0

v1 whole, which is shorter than its diff:
```python
import jax
import jax.numpy as jnp
from jax import lax
from jax.experimental import pallas as pl
from jax.experimental.pallas import tpu as pltpu
from jax.sharding import PartitionSpec as P

MESH = pl.DeviceIdType.MESH
F32, BF16 = jnp.float32, jnp.bfloat16
NY, NX, NZ = 4, 4, 8
N = 6
CW = 256
QUARTER = N * CW
KD = 768
ROWS = 16
OWN = 192
C1 = 0.7978845608028654
C2 = 0.044715


def remote(src, dst, sems, index, device):
    send, recv = sems
    return pltpu.make_async_remote_copy(
        src_ref=src, dst_ref=dst, send_sem=send.at[index], recv_sem=recv.at[index],
        device_id=device, device_id_type=MESH,
    )


def kernel(
    tok, wt, cot, hid, out,
    T, TT, Wv, Pf, Pb, Rc, S32, SB, R1, R2, G, GS, C, H, WG,
    tx_s, tx_r, ty_s, ty_r, tf_s, tf_r, pc_s, pc_r, rs_s, rs_r, yt_s, yt_r, ag_s, ag_r,
    gc_s, gc_r, wo_s, wo_r, w_sem, l_sem, o_sem,
):
    y, x, g = lax.axis_index("dp"), lax.axis_index("depth"), lax.axis_index("grid")
    z, c = g // 2, g % 2
    d = 1 - 2 * c

    def zmod(k):
        return (z + k + NZ) % NZ

    def at_z(k):
        return (y, x, zmod(k) * 2 + c)

    def at_x(k):
        return (y, (x + k) % NX, g)

    def at_y(k):
        return ((y + k) % NY, x, g)

    other = (y, x, z * 2 + 1 - c)

    own_tok = T.at[y, pl.ds(x * 4, 4)]
    tok_copy = pltpu.make_async_copy(tok, own_tok, l_sem.at[0])
    tok_copy.start()

    def w_copy(j, q):
        columns = pl.ds(pl.multiple_of(q * QUARTER + j * CW, CW), CW)
        return pltpu.make_async_copy(wt.at[:, columns], Wv.at[j, q], w_sem.at[j, q])

    for q in range(NY):
        w_copy(0, q).start()
    cot_copy = pltpu.make_async_copy(cot, C, l_sem.at[1])
    cot_copy.start()

    barrier = pltpu.get_barrier_semaphore()
    peers = [at_x(k) for k in (1, 2, 3)] + [at_y(k) for k in (1, 2, 3)]
    peers += [at_z(k) for k in (1, -1, 2, -2)] + [other]
    for peer in peers:
        pl.semaphore_signal(barrier, inc=1, device_id=peer, device_id_type=MESH)
    tok_copy.wait()
    pl.semaphore_wait(barrier, len(peers))

    def tok_x(k):
        return remote(own_tok, own_tok, (tx_s, tx_r), k - 1, at_x(k))

    def tok_x_in(k):
        here = T.at[y, pl.ds((x + NX - k) % NX * 4, 4)]
        return remote(here, here, (tx_s, tx_r), k - 1, at_x(k))

    def tok_y(k):
        return remote(own_tok, own_tok, (ty_s, ty_r), k - 1, at_y(k))

    def tok_y_in(k):
        here = T.at[(y + NY - k) % NY, pl.ds(x * 4, 4)]
        return remote(here, here, (ty_s, ty_r), k - 1, at_y(k))

    def tok_f(k, n):
        here = T.at[(y + NY - k) % NY, pl.ds(x * 4, 4)]
        return remote(here, here, (tf_s, tf_r), (k - 1, n - 1), at_x(n))

    def tok_f_in(k, n):
        here = T.at[(y + NY - k) % NY, pl.ds((x + NX - n) % NX * 4, 4)]
        return remote(here, here, (tf_s, tf_r), (k - 1, n - 1), at_x(n))

    for k in (2, 1, 3):
        tok_x(k).start()
    for k in (1, 3, 2):
        tok_y(k).start()

    @pl.loop(1, N)
    def _(j):
        for q in range(NY):
            w_copy(j, q).start()

    cot_copy.wait()
    for k in (1, 3, 2):
        tok_x_in(k).wait_recv()

    def pc(j):
        return remote(Pb.at[j, 1 - c], Rc.at[j], (pc_s, pc_r), j, other)

    def rs(j, n):
        sems = (rs_s, rs_r)
        if n == 0:
            return remote(SB.at[j, zmod(4)], R1.at[j, 0], sems, (j, 0), at_z(-2 * d))
        if n == 1:
            return remote(SB.at[j, zmod(-3 * d)], R1.at[j, 1], sems, (j, 1), at_z(-d))
        if n == 2:
            return remote(SB.at[j, zmod(3 * d)], R1.at[j, 2], sems, (j, 2), at_z(d))
        if n == 3:
            return remote(SB.at[j, zmod(-d)], R2.at[j, 0], sems, (j, 3), at_z(-d))
        if n == 4:
            return remote(SB.at[j, zmod(d)], R2.at[j, 1], sems, (j, 4), at_z(d))
        if n == 5:
            return remote(SB.at[j, zmod(-2 * d)], R2.at[j, 2], sems, (j, 5), at_z(-2 * d))
        return remote(SB.at[j, zmod(2 * d)], R2.at[j, 3], sems, (j, 6), at_z(2 * d))

    def yt(j, k):
        return remote(GS.at[j, (y + k) % NY], G.at[j, y, z, c], (yt_s, yt_r), (j, k - 1), at_y(k))

    def yt_in(j, k):
        here = G.at[j, (y + NY - k) % NY, z, c]
        return remote(here, here, (yt_s, yt_r), (j, k - 1), at_y(k))

    AG = ((0, 1), (0, -1), (0, 2), (0, -2), (-2, 1), (-2, 2), (2, -1))

    def ag(j, n):
        origin, to = AG[n]
        piece = G.at[j, :, zmod(origin * d), c]
        return remote(piece, piece, (ag_s, ag_r), (j, n), at_z(to * d))

    def ag_in(j, n):
        origin, to = AG[n]
        piece = G.at[j, :, zmod((origin - to) * d), c]
        return remote(piece, piece, (ag_s, ag_r), (j, n), at_z(to * d))

    def gc(j):
        piece = G.at[j, :, :, c]
        return remote(piece, piece, (gc_s, gc_r), j, other)

    def gc_in(j):
        piece = G.at[j, :, :, 1 - c]
        return remote(piece, piece, (gc_s, gc_r), j, other)

    def out_columns(group, j):
        return out.at[:, pl.ds(pl.multiple_of(group * QUARTER + j * CW, CW), CW)]

    def wo(j, k):
        return remote(WG.at[j, k], out_columns(y, j), (wo_s, wo_r), (j, k - 1), at_y(k))

    def wo_in(j, k):
        here = out_columns((y + NY - k) % NY, j)
        return remote(WG.at[j, k], here, (wo_s, wo_r), (j, k - 1), at_y(k))

    def wo_own(j):
        return pltpu.make_async_copy(WG.at[j, 0], out_columns(y, j), o_sem.at[j])

    def project(j):
        slot = j % 2
        rows = T[y].reshape(NZ * 2 * ROWS, KD)
        for q in range(NY):
            w_copy(j, q).wait()
            part = jnp.dot(rows, Wv[j, q], preferred_element_type=F32)
            part = part.reshape(NZ, 2, ROWS, CW)
            for core in range(2):
                Pf[slot, core, :, q] = part[:, core]
                Pb[j, core, :, q] = part[:, core].astype(BF16)
        pc(j).start()

    def reduce_first(j):
        pc(j).wait_recv()
        both = Pf[j % 2, c] + Rc[j].astype(F32)
        S32[j] = both
        SB[j] = both.astype(BF16)
        for n in (0, 1, 2, 3, 4):
            rs(j, n).start()

    def reduce_second(j):
        for n in (0, 1, 2):
            rs(j, n).wait_recv()
        near, far = zmod(-2 * d), zmod(2 * d)
        SB[j, near] = (S32[j, near] + R1[j, 0].astype(F32) + R1[j, 1].astype(F32)).astype(BF16)
        rs(j, 5).start()
        SB[j, far] = (S32[j, far] + R1[j, 2].astype(F32)).astype(BF16)
        rs(j, 6).start()

    def activate(j):
        for n in (3, 4, 5, 6):
            rs(j, n).wait_recv()
        v = S32[j, z] + R2[j, 0].astype(F32) + R2[j, 1].astype(F32)
        v = v + R2[j, 2].astype(F32) + R2[j, 3].astype(F32)
        square = v * v
        t = jnp.tanh(C1 * (v + C2 * (v * square)))
        half = 0.5 * (1.0 + t)
        slope = half + 0.5 * v * (1.0 - t * t) * (C1 * (1.0 + 3.0 * C2 * square))
        hidden = (v * half).astype(BF16)
        for q in range(NY):
            columns = pl.ds(pl.multiple_of(q * QUARTER + j * CW, CW), CW)
            H[:, columns] = hidden[q]
            GS[j, q] = (C[:, columns].astype(F32) * slope[q]).astype(BF16)
        for k in (2, 1, 3):
            yt(j, k).start()
        G[j, y, z, c] = GS[j, y]

    def gather_first(j):
        for k in (1, 3, 2):
            yt_in(j, k).wait_recv()
        for n in (2, 3, 0, 1):
            ag(j, n).start()

    def gather_second(j):
        ag_in(j, 2).wait_recv()
        ag(j, 5).start()
        ag(j, 4).start()
        ag_in(j, 3).wait_recv()
        ag(j, 6).start()

    def gather_cores(j):
        for n in (0, 1, 4, 5, 6):
            ag_in(j, n).wait_recv()
        gc(j).start()

    def weight_product(j):
        gc_in(j).wait_recv()
        for k in (2, 1, 3, 0):
            grad = G[j].reshape(NY * NZ * 2 * ROWS, CW)
            WG[j, k] = jnp.dot(TT[(y + k) % NY], grad, preferred_element_type=F32).astype(BF16)
            if k:
                wo(j, k).start()
            else:
                wo_own(j).start()

    def stage(j, run):
        pl.when(jnp.logical_and(j >= 0, j < N))(lambda: run(j))

    @pl.loop(-1, N + 5)
    def _(t):
        stage(t, reduce_first)

        @pl.when(t == 0)
        def _():
            for k in (1, 3, 2):
                tok_y_in(k).wait_recv()
                for n in (2, 1, 3):
                    tok_f(k, n).start()

        stage(t - 4, gather_second)
        stage(t - 1, reduce_second)
        stage(t - 3, gather_first)
        stage(t - 2, activate)
        stage(t - 5, gather_cores)
        stage(t + 1, project)

        @pl.when(jnp.logical_and(t >= 1, t <= 4))
        def _():
            k = t - 1

            @pl.when(k > 0)
            def _():
                for n in (1, 3, 2):
                    tok_f_in(k, n).wait_recv()

            group = (y + NY - k) % NY
            turned = T[group].reshape(NZ * 2 * ROWS, KD).T.reshape(NY, OWN, NZ * 2 * ROWS)
            TT[:, :, pl.ds(pl.multiple_of(group * 256, 256), 256)] = turned

        stage(t - 5, weight_product)

    hid_copy = pltpu.make_async_copy(H, hid, l_sem.at[2])
    hid_copy.start()
    for k in (1, 2, 3):
        tok_x(k).wait_send()
        tok_y(k).wait_send()
        for n in (1, 2, 3):
            tok_f(k, n).wait_send()

    @pl.loop(0, N)
    def _(j):
        pc(j).wait_send()
        gc(j).wait_send()
        for n in range(7):
            rs(j, n).wait_send()
            ag(j, n).wait_send()
        for k in (1, 2, 3):
            yt(j, k).wait_send()
            wo(j, k).wait_send()
            wo_in(j, k).wait_recv()
        wo_own(j).wait()

    hid_copy.wait()


def local(tokens, weight, cotangent):
    dma = pltpu.SemaphoreType.DMA
    piece = (NY, ROWS, CW)
    any_ref = pl.BlockSpec(memory_space=pl.ANY)
    pair = lambda *shape: [dma(shape), dma(shape)]
    hidden, grad = pl.pallas_call(
        kernel,
        out_shape=[
            jax.ShapeDtypeStruct(cotangent.shape, BF16),
            jax.ShapeDtypeStruct((OWN, weight.shape[1]), BF16),
        ],
        in_specs=[any_ref] * 3,
        out_specs=[any_ref] * 2,
        scratch_shapes=[
            pltpu.VMEM((NY, NZ * 2, ROWS, KD), BF16),
            pltpu.VMEM((NY, OWN, 1024), BF16),
            pltpu.VMEM((N, NY, KD, CW), BF16),
            pltpu.VMEM((2, 2, NZ) + piece, F32),
            pltpu.VMEM((N, 2, NZ) + piece, BF16),
            pltpu.VMEM((N, NZ) + piece, BF16),
            pltpu.VMEM((N, NZ) + piece, F32),
            pltpu.VMEM((N, NZ) + piece, BF16),
            pltpu.VMEM((N, 3) + piece, BF16),
            pltpu.VMEM((N, 4) + piece, BF16),
            pltpu.VMEM((N, NY, NZ, 2, ROWS, CW), BF16),
            pltpu.VMEM((N,) + piece, BF16),
            pltpu.VMEM(cotangent.shape, BF16),
            pltpu.VMEM(cotangent.shape, BF16),
            pltpu.VMEM((N, NY, OWN, CW), BF16),
            *pair(3), *pair(3), *pair(3, 3), *pair(N), *pair(N, 7), *pair(N, 3), *pair(N, 7),
            *pair(N), *pair(N, 3), dma((N, NY)), dma((3,)), dma((N,)),
        ],
        compiler_params=pltpu.CompilerParams(
            collective_id=0, has_side_effects=True, vmem_limit_bytes=56 * 2**20
        ),
        cost_estimate=pl.CostEstimate(
            flops=4 * 256 * 768 * 6144, bytes_accessed=13 * 2**20, transcendentals=16 * 6144
        ),
    )(tokens.reshape(4, ROWS, KD), weight, cotangent)
    return hidden, grad


def solution(mesh):
    return jax.shard_map(
        local,
        mesh=mesh,
        in_specs=(P(("dp", "depth"), "grid"), P("grid", "depth"), P(("dp", "grid"), "depth")),
        out_specs=(P(("dp", "grid"), "depth"), P(("grid", "dp"), "depth")),
        check_vma=False,
    )
```

time: 247 us -> 89.3 us (0.36)
  waiting for transfers between devices: 212 us -> 0 us
  Pallas kernels: 0 us -> 83.6 us
  matrix products: 18.1 us -> 0 us
  between operations: 13.8 us -> 0.64 us
  local copies, waits for them, and re-layouts: 0.01 us -> 4.91 us
    all_gather x2 -> x0, waiting for transfers between devices: 148 us -> none  [the longest x1 93.4 us: local(): lax.all_gather(grad_pre, ('dp', 'grid'), axis=0, tiled=True)]
    pallas_call x0 -> x1, Pallas kernels: none -> 83.6 us  [local(): pl.pallas_call(kernel, out_shape=[jax.ShapeDtypeStruct(cotangent.shape, B...]
    reduce_scatter x1 -> x0, waiting for transfers between devices: 64 us -> none  [local(): lax.psum_scatter(partial_pre, 'grid', scatter_dimension=0, tiled=True)]
    dot_general x2 -> x0, matrix products: 18.1 us -> none  [the longest x1 9.11 us: local(): partial_pre = jnp.dot(own_rows, weight, preferred_element_type=jnp.float32)]
    unnamed x2, local copies, waits for them, and re-layouts: 0.01 us -> 4.91 us
  transfers between devices with their start and end apart: 3 -> 0, of which waited for: 3 -> 0; matrix products, arithmetic and copies ran while one was open for 0% -> 0% of each run, Pallas kernels for 0% -> 0%
where the time goes in v1:
time: 89.3 us; the launch traced here: 89.1 us
  Pallas kernels  83.6 us (94%)
  local copies, waits for them, and re-layouts  4.91 us (5%)
    pallas_call x1, Pallas kernels, local(): pl.pallas_call(kernel, out_shape=[jax.ShapeDtypeStruct(cotangent.shape, B...  83.6 us
    unnamed x2, local copies, waits for them, and re-layouts  4.91 us

profile of v1, /device:TPU:1, one launch (start us, length us, event | category | flops | bytes accessed | tf_op | source)
XLA Modules:
  0.0 89.1 jit_solution(17759811202956355613)
XLA Ops:
  0.6 83.6 %shard_map.50 = (bf16[16,6144]{1,0:T(8,128)(2,1)}, bf16[192,6144]{1,0:T(8,128)(2,1)}) custom-call(bf16[4,16,768]{2,1,0:T(8,128)(2,1)} %bitcast.1, bf16[768,6144]{1,0:T(8,128)(2,1)} %wt.1, bf16[16,6144]{1,0:T(8,128)(2,1)} %cot.1), custom_call_target="tpu_custom_call" | custom-call | flops 4831838208 | bytes 13631488 | tf_op jit(solution)/shard_map/pallas_call | solution.py:309
  84.2 1.6 %copy.7 = bf16[16,6144]{1,0:T(8,128)(2,1)} copy(bf16[16,6144]{1,0:T(8,128)(2,1)} %get-tuple-element.4) | data formatting | bytes 393216
  85.8 3.3 %copy.8 = bf16[192,6144]{1,0:T(8,128)(2,1)} copy(bf16[192,6144]{1,0:T(8,128)(2,1)} %get-tuple-element.5) | data formatting | bytes 4718592

commit v2 on v1

--- a/solution.py
+++ b/solution.py
@@ -8,8 +8,12 @@
 MESH = pl.DeviceIdType.MESH
 F32, BF16 = jnp.float32, jnp.bfloat16
 NY, NX, NZ = 4, 4, 8
-N = 6
-CW = 256
+N = 12
+CW = 128
+AT = {"project": -5, "reduce_first": -4, "reduce_second": -1, "activate": 2, "gather_first": 4, "gather_second": 6, "gather_cores": 7, "weight_product": 8}
+ORDER = ["activate", "turn", "forward", "gather_second", "gather_first", "reduce_second", "weight_product", "project", "gather_cores", "reduce_first"]
+FORWARD = -3
+TURN = (0, 2, 5, 6)
 QUARTER = N * CW
 KD = 768
 ROWS = 16
@@ -50,6 +54,11 @@
 
     other = (y, x, z * 2 + 1 - c)
 
+    barrier = pltpu.get_barrier_semaphore()
+    peers = [at_x(2), at_y(2), at_z(2), at_z(-2), at_x(1), at_x(3), at_y(1), at_y(3), at_z(1), at_z(-1), other]
+    for peer in peers:
+        pl.semaphore_signal(barrier, inc=1, device_id=peer, device_id_type=MESH)
+
     own_tok = T.at[y, pl.ds(x * 4, 4)]
     tok_copy = pltpu.make_async_copy(tok, own_tok, l_sem.at[0])
     tok_copy.start()
@@ -63,11 +72,6 @@
     cot_copy = pltpu.make_async_copy(cot, C, l_sem.at[1])
     cot_copy.start()
 
-    barrier = pltpu.get_barrier_semaphore()
-    peers = [at_x(k) for k in (1, 2, 3)] + [at_y(k) for k in (1, 2, 3)]
-    peers += [at_z(k) for k in (1, -1, 2, -2)] + [other]
-    for peer in peers:
-        pl.semaphore_signal(barrier, inc=1, device_id=peer, device_id_type=MESH)
     tok_copy.wait()
     pl.semaphore_wait(barrier, len(peers))
 
@@ -167,7 +171,7 @@
         return pltpu.make_async_copy(WG.at[j, 0], out_columns(y, j), o_sem.at[j])
 
     def project(j):
-        slot = j % 2
+        slot = j % 3
         rows = T[y].reshape(NZ * 2 * ROWS, KD)
         for q in range(NY):
             w_copy(j, q).wait()
@@ -180,7 +184,7 @@
 
     def reduce_first(j):
         pc(j).wait_recv()
-        both = Pf[j % 2, c] + Rc[j].astype(F32)
+        both = Pf[j % 3, c] + Rc[j].astype(F32)
         S32[j] = both
         SB[j] = both.astype(BF16)
         for n in (0, 1, 2, 3, 4):
@@ -241,41 +245,51 @@
             else:
                 wo_own(j).start()
 
-    def stage(j, run):
-        pl.when(jnp.logical_and(j >= 0, j < N))(lambda: run(j))
-
-    @pl.loop(-1, N + 5)
-    def _(t):
-        stage(t, reduce_first)
-
-        @pl.when(t == 0)
-        def _():
-            for k in (1, 3, 2):
-                tok_y_in(k).wait_recv()
-                for n in (2, 1, 3):
-                    tok_f(k, n).start()
-
-        stage(t - 4, gather_second)
-        stage(t - 1, reduce_second)
-        stage(t - 3, gather_first)
-        stage(t - 2, activate)
-        stage(t - 5, gather_cores)
-        stage(t + 1, project)
-
-        @pl.when(jnp.logical_and(t >= 1, t <= 4))
-        def _():
-            k = t - 1
-
-            @pl.when(k > 0)
-            def _():
+    def retire(j):
+        pc(j).wait_send()
+        gc(j).wait_send()
+        for n in range(7):
+            rs(j, n).wait_send()
+            ag(j, n).wait_send()
+        for k in (1, 2, 3):
+            yt(j, k).wait_send()
+
+    def forward(t):
+        for k in (1, 3, 2):
+            tok_y_in(k).wait_recv()
+            for n in (2, 1, 3):
+                tok_f(k, n).start()
+
+    def turn(t):
+        def run(k):
+            if k:
                 for n in (1, 3, 2):
                     tok_f_in(k, n).wait_recv()
-
             group = (y + NY - k) % NY
             turned = T[group].reshape(NZ * 2 * ROWS, KD).T.reshape(NY, OWN, NZ * 2 * ROWS)
             TT[:, :, pl.ds(pl.multiple_of(group * 256, 256), 256)] = turned
 
-        stage(t - 5, weight_product)
+        for k in range(NY):
+            pl.when(t == TURN[k])(lambda k=k: run(k))
+
+    stages = {
+        "project": project, "reduce_first": reduce_first, "reduce_second": reduce_second,
+        "activate": activate, "gather_first": gather_first, "gather_second": gather_second,
+        "gather_cores": gather_cores, "weight_product": weight_product, "retire": retire,
+    }
+
+    at = dict(AT, retire=AT["weight_product"] + 1)
+
+    @pl.loop(min(AT.values()), N + AT["weight_product"])
+    def _(t):
+        for name in ORDER + ["retire"]:
+            if name == "forward":
+                pl.when(t == FORWARD)(lambda: forward(t))
+            elif name == "turn":
+                turn(t)
+            else:
+                j = t - at[name]
+                pl.when(jnp.logical_and(j >= 0, j < N))(lambda run=stages[name], j=j: run(j))
 
     hid_copy = pltpu.make_async_copy(H, hid, l_sem.at[2])
     hid_copy.start()
@@ -285,20 +299,32 @@
         for n in (1, 2, 3):
             tok_f(k, n).wait_send()
 
+    retire(N - 1)
+
     @pl.loop(0, N)
     def _(j):
-        pc(j).wait_send()
-        gc(j).wait_send()
-        for n in range(7):
-            rs(j, n).wait_send()
-            ag(j, n).wait_send()
         for k in (1, 2, 3):
-            yt(j, k).wait_send()
             wo(j, k).wait_send()
             wo_in(j, k).wait_recv()
         wo_own(j).wait()
 
     hid_copy.wait()
+
+
+def place(hidden, grad, hidden_out, grad_out, H, W, sem_in, sem_out):
+    parts = [(hidden, H, hidden_out)]
+    for n in range(6):
+        rows = pl.ds(n * 32, 32)
+        parts.append((grad.at[rows], W.at[rows], grad_out.at[rows]))
+    come = [pltpu.make_async_copy(p[0], p[1], sem_in.at[n]) for n, p in enumerate(parts)]
+    go = [pltpu.make_async_copy(p[1], p[2], sem_out.at[n]) for n, p in enumerate(parts)]
+    for copy in come:
+        copy.start()
+    for one, two in zip(come, go):
+        one.wait()
+        two.start()
+    for copy in go:
+        copy.wait()
 
 
 def local(tokens, weight, cotangent):
@@ -312,13 +338,13 @@
             jax.ShapeDtypeStruct(cotangent.shape, BF16),
             jax.ShapeDtypeStruct((OWN, weight.shape[1]), BF16),
         ],
-        in_specs=[any_ref] * 3,
+        in_specs=[pl.BlockSpec(memory_space=pltpu.HBM)] * 3,
         out_specs=[any_ref] * 2,
         scratch_shapes=[
             pltpu.VMEM((NY, NZ * 2, ROWS, KD), BF16),
             pltpu.VMEM((NY, OWN, 1024), BF16),
             pltpu.VMEM((N, NY, KD, CW), BF16),
-            pltpu.VMEM((2, 2, NZ) + piece, F32),
+            pltpu.VMEM((3, 2, NZ) + piece, F32),
             pltpu.VMEM((N, 2, NZ) + piece, BF16),
             pltpu.VMEM((N, NZ) + piece, BF16),
             pltpu.VMEM((N, NZ) + piece, F32),
@@ -334,12 +360,12 @@
             *pair(N), *pair(N, 3), dma((N, NY)), dma((3,)), dma((N,)),
         ],
         compiler_params=pltpu.CompilerParams(
-            collective_id=0, has_side_effects=True, vmem_limit_bytes=56 * 2**20
+            collective_id=0, has_side_effects=True, vmem_limit_bytes=51 * 2**20
         ),
         cost_estimate=pl.CostEstimate(
             flops=4 * 256 * 768 * 6144, bytes_accessed=13 * 2**20, transcendentals=16 * 6144
         ),
-    )(tokens.reshape(4, ROWS, KD), weight, cotangent)
+    )(*[pltpu.with_memory_space_constraint(a, pltpu.HBM) for a in (tokens.reshape(4, ROWS, KD), weight, cotangent)])
     return hidden, grad
 
 

time: 89.3 us -> 83.4 us (0.934)
  Pallas kernels: 83.6 us -> 80.6 us
  local copies, waits for them, and re-layouts: 4.91 us -> 2.08 us
    pallas_call x1, Pallas kernels: 83.6 us -> 80.6 us  [local(): pl.pallas_call(kernel, out_shape=[jax.ShapeDtypeStruct(cotangent.shape, B...]
    unnamed x2, local copies, waits for them, and re-layouts: 4.91 us -> 2.08 us
where the time goes in v2:
time: 83.4 us; the launch traced here: 83.3 us
  Pallas kernels  80.6 us (97%)
  local copies, waits for them, and re-layouts  2.08 us (2%)
    pallas_call x1, Pallas kernels, local(): pl.pallas_call(kernel, out_shape=[jax.ShapeDtypeStruct(cotangent.shape, B...  80.6 us
    unnamed x2, local copies, waits for them, and re-layouts  2.08 us

profile of v2, /device:TPU:1, one launch (start us, length us, event | category | flops | bytes accessed | tf_op | source)
XLA Modules:
  0.0 83.3 jit_solution(2950925703463024379)
XLA Ops:
  0.6 80.6 %shard_map.50 = (bf16[16,6144]{1,0:T(8,128)(2,1)S(1)}, bf16[192,6144]{1,0:T(8,128)(2,1)S(1)}) custom-call(bf16[4,16,768]{2,1,0:T(8,128)(2,1)} %bitcast.1, bf16[768,6144]{1,0:T(8,128)(2,1)} %wt.1, bf16[16,6144]{1,0:T(8,128)(2,1)} %cot.1), custom_call_target="tpu_custom_call" | custom-call | flops 4831838208 | bytes 13631488 | tf_op jit(solution)/shard_map/pallas_call | solution.py:335
  81.3 0.7 copy.7
  81.9 1.4 %copy.8 = bf16[192,6144]{1,0:T(8,128)(2,1)} copy(bf16[192,6144]{1,0:T(8,128)(2,1)S(1)} %get-tuple-element.5) | data formatting | bytes 4718592

commit v3 on v2

v3 whole, which is shorter than its diff:
```python
import jax
import jax.numpy as jnp
from jax import lax
from jax.experimental import pallas as pl
from jax.experimental.pallas import tpu as pltpu
from jax.sharding import PartitionSpec as P

MESH = pl.DeviceIdType.MESH
F32, BF16 = jnp.float32, jnp.bfloat16
NY, NX, NZ = 4, 4, 8
N = 12
CW = 128
AT = {"project": -5, "reduce_first": -4, "reduce_second": -1, "activate": 2, "gather_first": 4, "gather_second": 6, "gather_cores": 7, "weight_product": 8}
ORDER = ["activate", "turn", "forward", "gather_second", "gather_first", "reduce_second", "weight_product", "project", "gather_cores", "reduce_first"]
FORWARD = -3
TURN = (0, 2, 5, 6)
QUARTER = N * CW
KD = 768
ROWS = 16
OWN = 192
C1 = 0.7978845608028654
C2 = 0.044715


TX, TY, TF, PC, RS, YT, AGS, GC, WO = range(9)


def kernel(
    tok, wt, cot, hid, out,
    T, TT, Wv, Pf, Pb, Rc, S32, SB, R1, R2, G, GS, C, H, WG,
    send, tx_r, ty_r, tf_r, pc_r, ra_r, rb_r, yt_r, ag_r, gc_r, wo_r, w_sem, l_sem, o_sem,
):
    y, x, g = lax.axis_index("dp"), lax.axis_index("depth"), lax.axis_index("grid")
    z, c = g // 2, g % 2
    d = 1 - 2 * c

    def zmod(k):
        return (z + k + NZ) % NZ

    def at_z(k):
        return (y, x, zmod(k) * 2 + c)

    def at_x(k):
        return (y, (x + k) % NX, g)

    def at_y(k):
        return ((y + k) % NY, x, g)

    other = (y, x, z * 2 + 1 - c)

    def remote(src, dst, kind, recv, device):
        return pltpu.make_async_remote_copy(
            src_ref=src, dst_ref=dst, send_sem=send.at[kind], recv_sem=recv,
            device_id=device, device_id_type=MESH,
        )

    def arrived(like, recv):
        remote(like, like, 0, recv, other).wait_recv()

    def sent(like, kind):
        remote(like, like, kind, tx_r.at[0], other).wait_send()

    barrier = pltpu.get_barrier_semaphore()
    peers = [at_x(2), at_y(2), at_z(2), at_z(-2), at_x(1), at_x(3), at_y(1), at_y(3), at_z(1), at_z(-1), other]
    for peer in peers:
        pl.semaphore_signal(barrier, inc=1, device_id=peer, device_id_type=MESH)

    own_tok = T.at[y, pl.ds(x * 4, 4)]
    tok_copy = pltpu.make_async_copy(tok, own_tok, l_sem.at[0])
    tok_copy.start()

    def w_copy(j, q):
        columns = pl.ds(pl.multiple_of(q * QUARTER + j * CW, CW), CW)
        return pltpu.make_async_copy(wt.at[:, columns], Wv.at[j, q], w_sem.at[j])

    for q in range(NY):
        w_copy(0, q).start()
    cot_copy = pltpu.make_async_copy(cot, C, l_sem.at[1])
    cot_copy.start()

    tok_copy.wait()
    pl.semaphore_wait(barrier, len(peers))

    def tok_x(k):
        return remote(own_tok, own_tok, TX, tx_r.at[0], at_x(k))

    def tok_y(k):
        return remote(own_tok, own_tok, TY, ty_r.at[k - 1], at_y(k))

    def tok_f(k, n):
        here = T.at[(y + NY - k) % NY, pl.ds(x * 4, 4)]
        return remote(here, here, TF, tf_r.at[k - 1], at_x(n))

    three = T.at[0, pl.ds(0, 12)]

    for k in (2, 1, 3):
        tok_x(k).start()
    for k in (1, 3, 2):
        tok_y(k).start()

    @pl.loop(1, N)
    def _(j):
        for q in range(NY):
            w_copy(j, q).start()

    cot_copy.wait()
    arrived(three, tx_r.at[0])

    def pc(j):
        return remote(Pb.at[j, 1 - c], Rc.at[j], PC, pc_r.at[j], other)

    SUMS = ((4, -2, 0), (-3, -1, 1), (3, 1, 2), (-1, -1, 3), (1, 1, 4), (-2, -2, 5), (2, 2, 6))

    def rs(j, n):
        owner, to, place = SUMS[n]
        here, recv = (R1.at[j, place], ra_r) if place < 3 else (R2.at[j, place - 3], rb_r)
        return remote(SB.at[j, zmod(owner * d)], here, RS, recv.at[j], at_z(to * d))

    def yt(j, k):
        return remote(GS.at[j, (y + k) % NY], G.at[j, y, z, c], YT, yt_r.at[j], at_y(k))

    AG = ((0, 1), (0, -1), (0, 2), (0, -2), (-2, 1), (-2, 2), (2, -1))

    def ag(j, n):
        origin, to = AG[n]
        piece = G.at[j, :, zmod(origin * d), c]
        recv = ag_r.at[j, {2: 0, 3: 1}.get(n, 2)]
        return remote(piece, piece, AGS, recv, at_z(to * d))

    def gc(j):
        piece = G.at[j, :, :, c]
        return remote(piece, piece, GC, gc_r.at[j], other)

    def out_columns(group, j):
        return out.at[:, pl.ds(pl.multiple_of(group * QUARTER + j * CW, CW), CW)]

    def wo(j, k):
        return remote(WG.at[j, k], out_columns(y, j), WO, wo_r.at[0], at_y(k))

    def wo_own(j):
        return pltpu.make_async_copy(WG.at[j, 0], out_columns(y, j), o_sem.at[0])

    def project(j):
        slot = j % 3
        rows = T[y].reshape(NZ * 2 * ROWS, KD)
        pltpu.make_async_copy(Wv.at[j], Wv.at[j], w_sem.at[j]).wait()
        for q in range(NY):
            part = jnp.dot(rows, Wv[j, q], preferred_element_type=F32)
            part = part.reshape(NZ, 2, ROWS, CW)
            for core in range(2):
                Pf[slot, core, :, q] = part[:, core]
                Pb[j, core, :, q] = part[:, core].astype(BF16)
        pc(j).start()

    def reduce_first(j):
        arrived(Rc.at[j], pc_r.at[j])
        both = Pf[j % 3, c] + Rc[j].astype(F32)
        S32[j] = both
        SB[j] = both.astype(BF16)
        for n in (0, 1, 2, 3, 4):
            rs(j, n).start()

    def reduce_second(j):
        arrived(R1.at[j], ra_r.at[j])
        near, far = zmod(-2 * d), zmod(2 * d)
        SB[j, near] = (S32[j, near] + R1[j, 0].astype(F32) + R1[j, 1].astype(F32)).astype(BF16)
        rs(j, 5).start()
        SB[j, far] = (S32[j, far] + R1[j, 2].astype(F32)).astype(BF16)
        rs(j, 6).start()

    def activate(j):
        arrived(R2.at[j], rb_r.at[j])
        v = S32[j, z] + R2[j, 0].astype(F32) + R2[j, 1].astype(F32)
        v = v + R2[j, 2].astype(F32) + R2[j, 3].astype(F32)
        square = v * v
        t = jnp.tanh(C1 * (v + C2 * (v * square)))
        half = 0.5 * (1.0 + t)
        slope = half + 0.5 * v * (1.0 - t * t) * (C1 * (1.0 + 3.0 * C2 * square))
        hidden = (v * half).astype(BF16)
        for q in range(NY):
            columns = pl.ds(pl.multiple_of(q * QUARTER + j * CW, CW), CW)
            H[:, columns] = hidden[q]
            GS[j, q] = (C[:, columns].astype(F32) * slope[q]).astype(BF16)
        for k in (2, 1, 3):
            yt(j, k).start()
        G[j, y, z, c] = GS[j, y]

    def gather_first(j):
        arrived(GS.at[j, pl.ds(0, 3)], yt_r.at[j])
        for n in (2, 3, 0, 1):
            ag(j, n).start()

    def gather_second(j):
        arrived(SB.at[j, 0], ag_r.at[j, 0])
        ag(j, 5).start()
        ag(j, 4).start()
        arrived(SB.at[j, 0], ag_r.at[j, 1])
        ag(j, 6).start()

    def gather_cores(j):
        arrived(SB.at[j, pl.ds(0, 5)], ag_r.at[j, 2])
        gc(j).start()

    def weight_product(j):
        arrived(G.at[j, :, :, 1 - c], gc_r.at[j])
        for k in (2, 1, 3, 0):
            grad = G[j].reshape(NY * NZ * 2 * ROWS, CW)
            WG[j, k] = jnp.dot(TT[(y + k) % NY], grad, preferred_element_type=F32).astype(BF16)
            if k:
                wo(j, k).start()
            else:
                wo_own(j).start()

    def forward(t):
        for k in (1, 3, 2):
            arrived(own_tok, ty_r.at[k - 1])
            for n in (2, 1, 3):
                tok_f(k, n).start()

    def turn(t):
        def run(k):
            if k:
                arrived(three, tf_r.at[k - 1])
            group = (y + NY - k) % NY
            turned = T[group].reshape(NZ * 2 * ROWS, KD).T.reshape(NY, OWN, NZ * 2 * ROWS)
            TT[:, :, pl.ds(pl.multiple_of(group * 256, 256), 256)] = turned

        for k in range(NY):
            pl.when(t == TURN[k])(lambda k=k: run(k))

    stages = {
        "project": project, "reduce_first": reduce_first, "reduce_second": reduce_second,
        "activate": activate, "gather_first": gather_first, "gather_second": gather_second,
        "gather_cores": gather_cores, "weight_product": weight_product,
    }

    @pl.loop(min(AT.values()), N + AT["weight_product"])
    def _(t):
        for name in ORDER:
            if name == "forward":
                pl.when(t == FORWARD)(lambda: forward(t))
            elif name == "turn":
                turn(t)
            else:
                j = t - AT[name]
                pl.when(jnp.logical_and(j >= 0, j < N))(lambda run=stages[name], j=j: run(j))

    hid_copy = pltpu.make_async_copy(H, hid, l_sem.at[2])
    hid_copy.start()
    sent(three, TX)
    sent(three, TY)
    sent(T.at[pl.ds(0, 3), pl.ds(0, 12)], TF)
    sent(Pb.at[:, 0], PC)
    sent(SB.at[:, pl.ds(0, 7)], RS)
    sent(GS.at[:, pl.ds(0, 3)], YT)
    sent(SB.at[:, pl.ds(0, 7)], AGS)
    sent(G.at[:, :, :, 0], GC)
    sent(WG.at[:, pl.ds(0, 3)], WO)
    arrived(WG.at[:, pl.ds(0, 3)], wo_r.at[0])
    pltpu.make_async_copy(WG.at[:, 0], WG.at[:, 0], o_sem.at[0]).wait()
    hid_copy.wait()


def place(hidden, grad, hidden_out, grad_out, H, W, sem_in, sem_out):
    parts = [(hidden, H, hidden_out)]
    for n in range(6):
        rows = pl.ds(n * 32, 32)
        parts.append((grad.at[rows], W.at[rows], grad_out.at[rows]))
    come = [pltpu.make_async_copy(p[0], p[1], sem_in.at[n]) for n, p in enumerate(parts)]
    go = [pltpu.make_async_copy(p[1], p[2], sem_out.at[n]) for n, p in enumerate(parts)]
    for copy in come:
        copy.start()
    for one, two in zip(come, go):
        one.wait()
        two.start()
    for copy in go:
        copy.wait()


def local(tokens, weight, cotangent):
    dma = pltpu.SemaphoreType.DMA
    piece = (NY, ROWS, CW)
    any_ref = pl.BlockSpec(memory_space=pl.ANY)
    hidden, grad = pl.pallas_call(
        kernel,
        out_shape=[
            jax.ShapeDtypeStruct(cotangent.shape, BF16),
            jax.ShapeDtypeStruct((OWN, weight.shape[1]), BF16),
        ],
        in_specs=[pl.BlockSpec(memory_space=pltpu.HBM)] * 3,
        out_specs=[any_ref] * 2,
        scratch_shapes=[
            pltpu.VMEM((NY, NZ * 2, ROWS, KD), BF16),
            pltpu.VMEM((NY, OWN, 1024), BF16),
            pltpu.VMEM((N, NY, KD, CW), BF16),
            pltpu.VMEM((3, 2, NZ) + piece, F32),
            pltpu.VMEM((N, 2, NZ) + piece, BF16),
            pltpu.VMEM((N, NZ) + piece, BF16),
            pltpu.VMEM((N, NZ) + piece, F32),
            pltpu.VMEM((N, NZ) + piece, BF16),
            pltpu.VMEM((N, 3) + piece, BF16),
            pltpu.VMEM((N, 4) + piece, BF16),
            pltpu.VMEM((N, NY, NZ, 2, ROWS, CW), BF16),
            pltpu.VMEM((N,) + piece, BF16),
            pltpu.VMEM(cotangent.shape, BF16),
            pltpu.VMEM(cotangent.shape, BF16),
            pltpu.VMEM((N, NY, OWN, CW), BF16),
            dma((9,)), dma((1,)), dma((3,)), dma((3,)), dma((N,)), dma((N,)), dma((N,)), dma((N,)),
            dma((N, 3)), dma((N,)), dma((1,)), dma((N,)), dma((3,)), dma((1,)),
        ],
        compiler_params=pltpu.CompilerParams(
            collective_id=0, has_side_effects=True, vmem_limit_bytes=51 * 2**20
        ),
        cost_estimate=pl.CostEstimate(
            flops=4 * 256 * 768 * 6144, bytes_accessed=13 * 2**20, transcendentals=16 * 6144
        ),
    )(*[pltpu.with_memory_space_constraint(a, pltpu.HBM) for a in (tokens.reshape(4, ROWS, KD), weight, cotangent)])
    return hidden, grad


def solution(mesh):
    return jax.shard_map(
        local,
        mesh=mesh,
        in_specs=(P(("dp", "depth"), "grid"), P("grid", "depth"), P(("dp", "grid"), "depth")),
        out_specs=(P(("dp", "grid"), "depth"), P(("grid", "dp"), "depth")),
        check_vma=False,
    )
```

time: 83.4 us -> 77.3 us (0.927)
  Pallas kernels: 80.6 us -> 74.4 us
    pallas_call x1, Pallas kernels: 80.6 us -> 74.4 us  [local(): pl.pallas_call(kernel, out_shape=[jax.ShapeDtypeStruct(cotangent.shape, B...]
where the time goes in v3:
time: 77.3 us; the launch traced here: 77.2 us
  Pallas kernels  74.4 us (96%)
  local copies, waits for them, and re-layouts  2.08 us (3%)
    pallas_call x1, Pallas kernels, local(): pl.pallas_call(kernel, out_shape=[jax.ShapeDtypeStruct(cotangent.shape, B...  74.4 us
    unnamed x2, local copies, waits for them, and re-layouts  2.08 us

profile of v3, /device:TPU:1, one launch (start us, length us, event | category | flops | bytes accessed | tf_op | source)
XLA Modules:
  0.0 77.2 jit_solution(14513799857056414975)
XLA Ops:
  0.6 74.4 %shard_map.50 = (bf16[16,6144]{1,0:T(8,128)(2,1)S(1)}, bf16[192,6144]{1,0:T(8,128)(2,1)S(1)}) custom-call(bf16[4,16,768]{2,1,0:T(8,128)(2,1)} %bitcast.1, bf16[768,6144]{1,0:T(8,128)(2,1)} %wt.1, bf16[16,6144]{1,0:T(8,128)(2,1)} %cot.1), custom_call_target="tpu_custom_call" | custom-call | flops 4831838208 | bytes 13631488 | tf_op jit(solution)/shard_map/pallas_call | solution.py:284
  75.1 0.7 copy.7
  75.8 1.4 %copy.8 = bf16[192,6144]{1,0:T(8,128)(2,1)} copy(bf16[192,6144]{1,0:T(8,128)(2,1)S(1)} %get-tuple-element.5) | data formatting | bytes 4718592

commit v4 on v3

--- a/solution.py
+++ b/solution.py
@@ -261,19 +261,14 @@
     hid_copy.wait()
 
 
-def place(hidden, grad, hidden_out, grad_out, H, W, sem_in, sem_out):
-    parts = [(hidden, H, hidden_out)]
-    for n in range(6):
-        rows = pl.ds(n * 32, 32)
-        parts.append((grad.at[rows], W.at[rows], grad_out.at[rows]))
-    come = [pltpu.make_async_copy(p[0], p[1], sem_in.at[n]) for n, p in enumerate(parts)]
-    go = [pltpu.make_async_copy(p[1], p[2], sem_out.at[n]) for n, p in enumerate(parts)]
-    for copy in come:
+def place(hidden, grad, hidden_out, grad_out, sems):
+    copies = [pltpu.make_async_copy(hidden, hidden_out, sems.at[0])]
+    for n in range(4):
+        rows = pl.ds(n * 48, 48)
+        copies.append(pltpu.make_async_copy(grad.at[rows], grad_out.at[rows], sems.at[1 + n]))
+    for copy in copies:
         copy.start()
-    for one, two in zip(come, go):
-        one.wait()
-        two.start()
-    for copy in go:
+    for copy in copies:
         copy.wait()
 
 
@@ -315,7 +310,13 @@
             flops=4 * 256 * 768 * 6144, bytes_accessed=13 * 2**20, transcendentals=16 * 6144
         ),
     )(*[pltpu.with_memory_space_constraint(a, pltpu.HBM) for a in (tokens.reshape(4, ROWS, KD), weight, cotangent)])
-    return hidden, grad
+    return pl.pallas_call(
+        place,
+        out_shape=[jax.ShapeDtypeStruct(a.shape, BF16) for a in (hidden, grad)],
+        in_specs=[any_ref] * 2,
+        out_specs=[any_ref] * 2,
+        scratch_shapes=[dma((5,))],
+    )(*[pltpu.with_memory_space_constraint(a, pltpu.VMEM) for a in (hidden, grad)])
 
 
 def solution(mesh):

time: 77.3 us -> 76.7 us (level)
  local copies, waits for them, and re-layouts: 2.08 us -> 0 us
  Pallas kernels: 74.4 us -> 76 us
    unnamed x2 -> x0, local copies, waits for them, and re-layouts: 2.08 us -> none
    pallas_call x0 -> x1, Pallas kernels: none -> 1.51 us  [local(): pl.pallas_call(place, out_shape=[jax.ShapeDtypeStruct(a.shape, BF16) for...]
where the time goes in v4:
time: 76.7 us; the launch traced here: 76.6 us
  Pallas kernels  76 us (99%)
    pallas_call x1, Pallas kernels, local(): pl.pallas_call(kernel, out_shape=[jax.ShapeDtypeStruct(cotangent.shape, B...  74.4 us

profile of v4, /device:TPU:1, one launch (start us, length us, event | category | flops | bytes accessed | tf_op | source)
XLA Modules:
  0.0 76.6 jit_solution(11276332874297462745)
XLA Ops:
  0.6 74.4 %shard_map.50 = (bf16[16,6144]{1,0:T(8,128)(2,1)S(1)}, bf16[192,6144]{1,0:T(8,128)(2,1)S(1)}) custom-call(bf16[4,16,768]{2,1,0:T(8,128)(2,1)} %bitcast.1, bf16[768,6144]{1,0:T(8,128)(2,1)} %wt.1, bf16[16,6144]{1,0:T(8,128)(2,1)} %cot.1), custom_call_target="tpu_custom_call" | custom-call | flops 4831838208 | bytes 13631488 | tf_op jit(solution)/shard_map/pallas_call | solution.py:279
  75.1 1.5 %shard_map.51 = (bf16[16,6144]{1,0:T(8,128)(2,1)}, bf16[192,6144]{1,0:T(8,128)(2,1)}) custom-call(bf16[16,6144]{1,0:T(8,128)(2,1)S(1)} %get-tuple-element.4.hidden, bf16[192,6144]{1,0:T(8,128)(2,1)S(1)} %get-tuple-element.5.grad), custom_call_target="tpu_custom_call" | custom-call | tf_op jit(solution)/shard_map/pallas_call | solution.py:313

commit v5 on v4

--- a/solution.py
+++ b/solution.py
@@ -187,7 +187,7 @@
 
     def gather_first(j):
         arrived(GS.at[j, pl.ds(0, 3)], yt_r.at[j])
-        for n in (2, 3, 0, 1):
+        for n in (2, 3):
             ag(j, n).start()
 
     def gather_second(j):
@@ -196,6 +196,8 @@
         ag(j, 4).start()
         arrived(SB.at[j, 0], ag_r.at[j, 1])
         ag(j, 6).start()
+        ag(j, 0).start()
+        ag(j, 1).start()
 
     def gather_cores(j):
         arrived(SB.at[j, pl.ds(0, 5)], ag_r.at[j, 2])

time: 76.7 us -> 76.5 us (level)
  Pallas kernels: 76 us -> 75.2 us
where the time goes in v5:
time: 76.5 us; the launch traced here: 75.9 us
  Pallas kernels  75.2 us (98%)
    pallas_call x1, Pallas kernels, local(): pl.pallas_call(kernel, out_shape=[jax.ShapeDtypeStruct(cotangent.shape, B...  73.7 us

profile of v5, /device:TPU:1, one launch (start us, length us, event | category | flops | bytes accessed | tf_op | source)
XLA Modules:
  0.0 75.9 jit_solution(3017315335048326197)
XLA Ops:
  0.6 73.7 %shard_map.50 = (bf16[16,6144]{1,0:T(8,128)(2,1)S(1)}, bf16[192,6144]{1,0:T(8,128)(2,1)S(1)}) custom-call(bf16[4,16,768]{2,1,0:T(8,128)(2,1)} %bitcast.1, bf16[768,6144]{1,0:T(8,128)(2,1)} %wt.1, bf16[16,6144]{1,0:T(8,128)(2,1)} %cot.1), custom_call_target="tpu_custom_call" | custom-call | flops 4831838208 | bytes 13631488 | tf_op jit(solution)/shard_map/pallas_call | solution.py:281
  74.4 1.5 %shard_map.51 = (bf16[16,6144]{1,0:T(8,128)(2,1)}, bf16[192,6144]{1,0:T(8,128)(2,1)}) custom-call(bf16[16,6144]{1,0:T(8,128)(2,1)S(1)} %get-tuple-element.4.hidden, bf16[192,6144]{1,0:T(8,128)(2,1)S(1)} %get-tuple-element.5.grad), custom_call_target="tpu_custom_call" | custom-call | tf_op jit(solution)/shard_map/pallas_call | solution.py:315
